TPU v7x, 256 devices: a whole 4x4x8 slice. The times are simulated.
256 devices in a mesh: wide: 32 (over x_lo, z, core), narrow: 8 (over y, x_hi).
Axes of the slice: x: 4 (x_hi: 2, x_lo: 2; x = x_hi * 2 + x_lo), y: 4, z: 8, core: 2. Of those that a mesh axis runs over, the one named last changes fastest.
Arguments:
- activations: bfloat16 [256, 256, 32, 256], P('wide', 'narrow'), may hold values from -6 to 6
- cotangent: bfloat16 [256, 256, 32, 256], P('wide', 'narrow'), may hold values from -6 to 6
- point_weight: bfloat16 [32, 32], replicated, may hold values from -1 to 1
- bias: float32 [32], replicated, may hold values from -3 to 3
- spectral_weight: bfloat16 [2, 32, 32, 16, 32, 32], P(None, 'wide', 'narrow'), may hold values from -6 to 6
Outputs:
- input_grad: bfloat16 [256, 256, 32, 256], P('wide', 'narrow')
- point_grad: float32 [32, 32], replicated
- bias_grad: float32 [32], replicated
- spectral_grad: float32 [2, 32, 32, 16, 32, 32], P(None, 'wide', 'narrow')
All inputs are finite; a program needn't handle non-finite values.
Results may differ from a plain program's by a relative error of at most 0.0065.
Values sent between devices are 32-bit elements; how exact they have to be, the bound alone decides.
A program may use at most 128 MiB of HBM per device.

v0:
```python
import math
import jax
import jax.numpy as jnp
from jax import lax
from jax.sharding import PartitionSpec as P

M = 16


def contract(form, left, right):
    return jnp.einsum(
        form, left, right, precision=lax.Precision.HIGH, preferred_element_type=jnp.float32
    )


def precise_product(form, left, right):
    return jnp.einsum(
        form, left, right, precision=lax.Precision.HIGHEST, preferred_element_type=jnp.float32
    )


def kept_freq(index, length, half):
    return jnp.where(index < half, index, length - 2 * half + index)


def phase_tables(freqs, cells, length):
    product = freqs[:, None] * cells[None, :] % length
    angle = product.astype(jnp.float32) * (2.0 * math.pi / length)
    return (jnp.cos(angle), jnp.sin(angle))


def rotate(real_part, imag_part, cosine, sine, sign_value, form):
    first = contract(form, real_part, cosine) - sign_value * contract(form, imag_part, sine)
    second = contract(form, imag_part, cosine) + sign_value * contract(form, real_part, sine)
    return (first, second)


def depth_forward(field, modes):
    length = field.shape[3]
    cosine, sine = phase_tables(
        jnp.arange(modes, dtype=jnp.int32), jnp.arange(length, dtype=jnp.int32), length
    )
    real_part = contract("abcz,kz->abck", field, cosine)
    imag_part = -contract("abcz,kz->abck", field, sine)
    shape = (field.shape[0], field.shape[1], -1)
    return (real_part.reshape(shape), imag_part.reshape(shape))


def depth_inverse(real_part, imag_part, depth_weights, length):
    modes = depth_weights.shape[0]
    shape = (real_part.shape[0], real_part.shape[1], real_part.shape[2] // modes, modes)
    cosine, sine = phase_tables(
        jnp.arange(modes, dtype=jnp.int32), jnp.arange(length, dtype=jnp.int32), length
    )
    return contract(
        "abck,kz->abcz", real_part.reshape(shape), cosine * depth_weights[:, None]
    ) - contract("abck,kz->abcz", imag_part.reshape(shape), sine * depth_weights[:, None])


def mix_modes(coeffs, weight):
    lead_x, lead_y = (coeffs.shape[0], coeffs.shape[1])
    modes = weight.shape[3]
    split = coeffs.reshape(lead_x, lead_y, 2, -1, modes)
    factor = weight.astype(jnp.float32)
    real_part = precise_product("pqck,pqkco->pqok", split[:, :, 0], factor[0]) - precise_product(
        "pqck,pqkco->pqok", split[:, :, 1], factor[1]
    )
    imag_part = precise_product("pqck,pqkco->pqok", split[:, :, 0], factor[1]) + precise_product(
        "pqck,pqkco->pqok", split[:, :, 1], factor[0]
    )
    return jnp.stack((real_part, imag_part), axis=2).reshape(lead_x, lead_y, 2, -1)


def weight_terms(coeffs, grads, weight):
    lead_x, lead_y = (coeffs.shape[0], coeffs.shape[1])
    modes = weight.shape[3]
    split_c = coeffs.reshape(lead_x, lead_y, 2, -1, modes)
    split_g = grads.reshape(lead_x, lead_y, 2, -1, modes)
    form = "pqck,pqok->pqkco"
    grad_real = precise_product(form, split_c[:, :, 0], split_g[:, :, 0]) + precise_product(
        form, split_c[:, :, 1], split_g[:, :, 1]
    )
    grad_imag = precise_product(form, split_c[:, :, 0], split_g[:, :, 1]) - precise_product(
        form, split_c[:, :, 1], split_g[:, :, 0]
    )
    factor = weight.astype(jnp.float32)
    back = "pqok,pqkco->pqck"
    back_real = precise_product(back, split_g[:, :, 0], factor[0]) + precise_product(
        back, split_g[:, :, 1], factor[1]
    )
    back_imag = precise_product(back, split_g[:, :, 1], factor[0]) - precise_product(
        back, split_g[:, :, 0], factor[1]
    )
    coeff_grad = jnp.stack((back_real, back_imag), axis=2).reshape(lead_x, lead_y, 2, -1)
    return (jnp.stack((grad_real, grad_imag), axis=0), coeff_grad)


def local(activations, cotangent, point_weight, bias, spectral_weight):
    size_x = lax.axis_size("wide")
    size_y = lax.axis_size("narrow")
    rows_x, rows_y, channels, length = activations.shape
    span_x = rows_x * size_x
    span_y = rows_y * size_y
    scale = 1.0 / math.sqrt(span_x * span_y * length)
    local_x = 2 * M // size_x
    local_y = 2 * M // size_y
    features = channels * M
    cells_x = lax.axis_index("wide") * rows_x + jnp.arange(rows_x, dtype=jnp.int32)
    cells_y = lax.axis_index("narrow") * rows_y + jnp.arange(rows_y, dtype=jnp.int32)
    all_modes = jnp.arange(2 * M, dtype=jnp.int32)
    depth_weights = jnp.where(jnp.arange(M, dtype=jnp.int32) == 0, 1.0, 2.0).astype(jnp.float32)
    unit_weights = jnp.ones((M,), jnp.float32)

    def to_modes(field):
        real_part, imag_part = depth_forward(field, M)
        cos_y, sin_y = phase_tables(kept_freq(all_modes, span_y, M), cells_y, span_y)
        cos_x, sin_x = phase_tables(kept_freq(all_modes, span_x, M), cells_x, span_x)
        re_y, im_y = rotate(real_part, imag_part, cos_y, sin_y, -1.0, "ayf,ky->kaf")
        re_x, im_x = rotate(re_y, im_y, cos_x, sin_x, -1.0, "qaf,ka->kqf")
        full = jnp.stack((re_x, im_x), axis=2)
        blocked = (
            full.reshape(size_x, local_x, size_y, local_y, 2, features)
            .transpose(0, 2, 1, 3, 4, 5)
            .reshape(4 * M * M, 2, features)
        )
        result = lax.psum_scatter(
            blocked, ("wide", "narrow"), scatter_dimension=0, tiled=True
        ).reshape(local_x, local_y, 2, features)
        return result * scale

    def to_field(modes, weights_here):
        whole = lax.all_gather(
            modes.reshape(local_x * local_y, 2, features), ("wide", "narrow"), axis=0, tiled=True
        )
        ordered = (
            whole.reshape(size_x, size_y, local_x, local_y, 2, features)
            .transpose(0, 2, 1, 3, 4, 5)
            .reshape(2 * M, 2 * M, 2, features)
        )
        cos_x, sin_x = phase_tables(kept_freq(all_modes, span_x, M), cells_x, span_x)
        cos_y, sin_y = phase_tables(kept_freq(all_modes, span_y, M), cells_y, span_y)
        re_x, im_x = rotate(ordered[:, :, 0], ordered[:, :, 1], cos_x, sin_x, 1.0, "kqf,ka->aqf")
        real_part, imag_part = rotate(re_x, im_x, cos_y, sin_y, 1.0, "akf,ky->ayf")
        return depth_inverse(real_part, imag_part, weights_here, length) * scale

    coeffs = to_modes(activations)
    mixed = mix_modes(coeffs, spectral_weight)
    spectral = to_field(mixed, depth_weights)
    point = jnp.einsum(
        "abcz,co->aboz", activations, point_weight, preferred_element_type=jnp.float32
    )
    preact = spectral + point + bias[None, None, :, None]
    _, pullback = jax.vjp(jax.nn.gelu, preact)
    pre_grad = pullback(cotangent.astype(jnp.float32))[0].astype(jnp.bfloat16)
    grad_modes = to_modes(pre_grad)
    grads = (grad_modes.reshape(local_x, local_y, 2, channels, M) * depth_weights).reshape(
        local_x, local_y, 2, features
    )
    spectral_grad, coeff_grad = weight_terms(coeffs, grads, spectral_weight)
    back = to_field(coeff_grad, unit_weights)
    mixing_back = jnp.einsum(
        "aboz,co->abcz", pre_grad, point_weight, preferred_element_type=jnp.float32
    )
    input_grad = (mixing_back + back).astype(jnp.bfloat16)
    weight_sum = jnp.einsum(
        "abcz,aboz->co", activations, pre_grad, preferred_element_type=jnp.float32
    )
    bias_sum = jnp.sum(pre_grad.astype(jnp.float32), axis=(0, 1, 3))
    point_total, bias_total = lax.psum((weight_sum, bias_sum), ("wide", "narrow"))
    return (input_grad, point_total * scale, bias_total * scale, spectral_grad)


def solution(mesh):
    return jax.shard_map(
        local,
        mesh=mesh,
        in_specs=(
            P("wide", "narrow", None, None),
            P("wide", "narrow", None, None),
            P(),
            P(),
            P(None, "wide", "narrow", None, None, None),
        ),
        out_specs=(
            P("wide", "narrow", None, None),
            P(),
            P(),
            P(None, "wide", "narrow", None, None, None),
        ),
        check_vma=False,
    )
```

profile of v0, /device:TPU:99, one launch (start us, length us, event | category | flops | bytes accessed | tf_op | source)
XLA Modules:
  0.0 2125.2 jit_solution(8341795437255912561)
XLA Ops:
  7.2 9.2 negate_bitcast_fusion
  16.4 6.9 convolution_bitcast_fusion
  23.3 2.6 copy.102
  25.9 3.6 copy.99
  29.5 1.3 convolution_multiply_fusion.3
  31.1 1.3 convolution_multiply_fusion.2
  32.5 1.3 convolution_subtract_fusion.1
  33.8 1.3 convolution_add_fusion.1
  35.1 1.2 fusion.56
  36.3 1.2 fusion.60
  37.5 1.3 multiply_add_fusion.1
  38.8 1.2 copy.114
  40.0 1.3 multiply_subtract_fusion.1
  41.3 1.2 copy.111
  42.6 2.5 pad_maximum_fusion
  45.1 271.2 %all-reduce.6.cloned.1.call-done = f32[1024,2,512]{2,0,1:T(8,128)} async-done(((f32[1024,2,512]{2,0,1:T(8,128)}), f32[1024,2,512]{2,0,1:T(8,128)}) %all-reduce.6.cloned.1.call-update) | async-done | bytes 4194320
  317.3 1.3 fusion.32
  320.1 6.7 fusion.101
  326.8 703.0 %all-gather.3.cloned.1.call-done = f32[1024,2,512]{2,1,0:T(2,128)} async-done(((f32[4,2,512]{2,1,0:T(2,128)}), f32[1024,2,512]{2,1,0:T(2,128)}) %all-gather.3.cloned.1.call-update) | async-done | bytes 4194320 | tf_op jit(solution)/shard_map/all_gather | solution.py:132
  1029.8 3.0 copy.117
  1033.6 1.8 fusion.14
  1035.4 1.7 fusion.15
  1037.1 1.8 fusion.24
  1038.8 1.7 fusion.25
  1042.1 1.6 fusion.28
  1043.7 2.0 fusion.29
  1045.7 1.6 copy.122
  1047.3 2.4 copy.123
  1049.7 1.6 copy.126
  1051.3 2.4 copy.127
  1053.7 5.2 fusion.69
  1058.9 13.2 convert_reduce_fusion
  1072.2 6.9 convolution_negate_fusion
  1079.1 5.6 fusion.12
  1084.7 3.7 copy.132
  1088.3 2.9 convolution_multiply_fusion.1
  1091.3 1.3 convolution_multiply_fusion
  1092.6 1.3 convolution_subtract_fusion
  1094.2 1.3 convolution_add_fusion
  1095.5 1.2 fusion.44
  1096.7 1.2 fusion.48
  1097.9 1.3 multiply_add_fusion
  1099.2 1.2 copy.144
  1100.4 1.3 multiply_subtract_fusion
  1101.7 1.2 copy.141
  1103.0 2.4 pad_maximum_fusion.1
  1105.4 264.0 %all-reduce.8.cloned.1.call-done = f32[1024,2,512]{2,0,1:T(8,128)} async-done(((f32[1024,2,512]{2,0,1:T(8,128)}), f32[1024,2,512]{2,0,1:T(8,128)}) %all-reduce.8.cloned.1.call-update) | async-done | bytes 4194320
  1370.5 1.2 fusion.36
  1372.9 4.7 convolution_bitcast_fusion.1
  1377.5 72.7 %all-reduce.2 = (f32[32,32]{0,1:T(8,128)S(1)}, f32[32]{0:T(128)S(1)}) all-reduce(f32[32,32]{0,1:T(8,128)S(1)} %convolution_bitcast_fusion.1, f32[32]{0:T(128)S(1)} %get-tuple-element.40), channel_id=1, replica_groups=mesh['wide'=32,'narrow'=8] {'wide','narrow'}, use_global_device_ids=true, to_apply=%region_2.3 | all-reduce | flops 1056 | bytes 8448 | tf_op jit(solution)/shard_map/psum | solution.py:169
  1451.5 6.6 fusion.99
  1458.8 1.6 pad_maximum_fusion.2
  1460.3 623.1 %all-gather.5.cloned.1.call-done = f32[1024,2,512]{2,1,0:T(2,128)} async-done(((f32[4,2,512]{2,1,0:T(2,128)}), f32[1024,2,512]{2,1,0:T(2,128)}) %all-gather.5.cloned.1.call-update) | async-done | bytes 4194320 | tf_op jit(solution)/shard_map/all_gather | solution.py:132
  2083.4 3.0 copy.147
  2087.2 1.8 fusion.18
  2089.0 1.7 fusion.19
  2090.7 1.8 fusion.22
  2092.5 1.7 fusion.23
  2097.5 1.9 copy.152
  2099.4 2.6 copy.153
  2102.0 1.9 copy.156
  2104.0 3.4 copy.157
  2107.4 3.5 fusion.74
  2110.9 7.6 fusion.10
  (76 shorter events, 13.6 us)
Async XLA Ops:
  7.2 312.9 %copy-start = (bf16[32,32]{1,0:T(8,128)(2,1)S(1)}, bf16[32,32]{1,0:T(8,128)(2,1)}, u32[]{:S(2)}) copy-start(bf16[32,32]{1,0:T(8,128)(2,1)} %param.7) | copy-start | bytes 6148
  7.2 309.1 %all-reduce.6.cloned.1.call-start = ((), (), s32[]{:S(2)}) async-start(), calls=%async_computation.2 | async-start | bytes 8388608
  7.2 9.2 copy-start.1
  29.5 1.6 copy-start.4
  45.0 272.3 %copy-start.6 = (bf16[2,1,4,16,32,32]{5,4,3,2,1,0:T(8,128)(2,1)S(1)}, bf16[2,1,4,16,32,32]{5,4,3,2,1,0:T(8,128)(2,1)}, u32[]{:S(2)}) copy-start(bf16[2,1,4,16,32,32]{5,4,3,2,1,0:T(8,128)(2,1)} %param.9) | copy-start | bytes 786436
  45.0 984.8 %all-gather.3.cloned.1.call-start = ((), (), s32[]{:S(2)}) async-start(), calls=%async_computation | async-start | bytes 4210688 | tf_op jit(solution)/shard_map/all_gather | solution.py:132
  319.8 1049.6 %all-reduce.8.cloned.1.call-start = ((), (), s32[]{:S(2)}) async-start(), calls=%async_computation.3 | async-start | bytes 8388608
  1053.7 5.2 copy-start.7
  1053.7 5.3 copy-start.8
  1053.7 5.3 copy-start.9
  1072.2 6.9 copy-start.2
  1092.6 1.6 copy-start.3
  1105.4 978.0 %all-gather.5.cloned.1.call-start = ((), (), s32[]{:S(2)}) async-start(), calls=%async_computation.1 | async-start | bytes 4210688 | tf_op jit(solution)/shard_map/all_gather | solution.py:132
  2107.4 3.5 copy-start.5
Sparse Core Ops, SparseCore 0:
  45.2 271.0 all-reduce.5
  319.9 709.8 all-gather.2
  1105.5 263.8 all-reduce.7
  1373.0 710.3 all-gather.4
where the time goes:
time: 2130 us
  waiting for transfers between devices  1860 us (87%)
  matrix products  120 us (6%)
  blocking collectives  72.7 us (3%)
  local copies, waits for them, and re-layouts  44.2 us (2%)
    all_gather x2, waiting for transfers between devices, to_field(): lax.all_gather(modes.reshape(local_x * local_y, 2, features), ('wide', 'n...  1330 us
    unnamed x6, waiting for transfers between devices  535 us
    dot_general x40, matrix products, contract(): jnp.einsum(form, left, right, precision=lax.Precision.HIGH, preferred_ele...  102 us
    psum x1, blocking collectives, local(): lax.psum((weight_sum, bias_sum), ('wide', 'narrow'))  72.7 us
  transfers between devices with their start and end apart: 4, of which 4 were waited for; matrix products, arithmetic and copies ran while one was open for 1% of the time, Pallas kernels for 0%

commit v1 on v0

--- a/solution.py
+++ b/solution.py
@@ -129,8 +129,17 @@
         return result * scale
 
     def to_field(modes, weights_here):
-        whole = lax.all_gather(
-            modes.reshape(local_x * local_y, 2, features), ("wide", "narrow"), axis=0, tiled=True
+        whole = jnp.concatenate(
+            lax.all_to_all(
+                jnp.stack(
+                    [modes.reshape(local_x * local_y, 2, features)]
+                    * lax.axis_size(("wide", "narrow"))
+                ),
+                ("wide", "narrow"),
+                0,
+                0,
+            ),
+            axis=0,
         )
         ordered = (
             whole.reshape(size_x, size_y, local_x, local_y, 2, features)

time: 2130 us -> 993 us (0.47)
  waiting for transfers between devices: 1860 us -> 625 us
  blocking collectives: 72.7 us -> 130 us
  starting transfers between devices: 0.38 us -> 23.3 us
    all_gather x2 -> x0, waiting for transfers between devices: 1330 us -> none  [to_field(): lax.all_gather(modes.reshape(local_x * local_y, 2, features), ('wide', 'n...]
    all_to_all x0 -> x2, waiting for transfers between devices: none -> 87.1 us  [to_field(): lax.all_to_all(jnp.stack([modes.reshape(local_x * local_y, 2, features)]...]
    psum x1, blocking collectives: 72.7 us -> 130 us  [local(): lax.psum((weight_sum, bias_sum), ('wide', 'narrow'))]
    all_to_all x0 -> x2, starting transfers between devices: none -> 22.8 us  [to_field(): lax.all_to_all(jnp.stack([modes.reshape(local_x * local_y, 2, features)]...]
    unnamed x6 -> x4, waiting for transfers between devices: 535 us -> 538 us
  transfers between devices with their start and end apart: 4 -> 4, of which waited for: 4 -> 3; matrix products, arithmetic and copies ran while one was open for 1% -> 2% of each run, Pallas kernels for 0% -> 0%
where the time goes in v1:
time: 993 us; the launch traced here: 985 us
  waiting for transfers between devices  625 us (63%)
  blocking collectives  130 us (13%)
  matrix products  120 us (12%)
  local copies, waits for them, and re-layouts  59.5 us (6%)
  starting transfers between devices  23.3 us (2%)
  between operations  14.8 us (1%)
  other arithmetic  11.8 us (1%)
    unnamed x4, waiting for transfers between devices  538 us
    psum x1, blocking collectives, local(): lax.psum((weight_sum, bias_sum), ('wide', 'narrow'))  130 us
    dot_general x40, matrix products, contract(): jnp.einsum(form, left, right, precision=lax.Precision.HIGH, preferred_ele...  102 us
    all_to_all x2, waiting for transfers between devices, to_field(): lax.all_to_all(jnp.stack([modes.reshape(local_x * local_y, 2, features)]...  87.1 us
    all_to_all x2, starting transfers between devices, to_field(): lax.all_to_all(jnp.stack([modes.reshape(local_x * local_y, 2, features)]...  22.8 us
  transfers between devices with their start and end apart: 4, of which 3 were waited for; matrix products, arithmetic and copies ran while one was open for 2% of the time, Pallas kernels for 0%

profile of v1, /device:TPU:99, one launch (start us, length us, event | category | flops | bytes accessed | tf_op | source)
XLA Modules:
  0.0 984.8 jit_solution(8227948216992359902)
XLA Ops:
  7.2 9.2 negate_bitcast_fusion
  16.4 6.9 convolution_bitcast_fusion
  23.3 2.6 copy.104
  25.9 3.6 copy.101
  29.5 1.3 convolution_multiply_fusion.3
  31.1 1.3 convolution_multiply_fusion.2
  32.5 1.3 convolution_subtract_fusion.1
  33.8 1.3 convolution_add_fusion.1
  36.3 1.2 fusion.60
  37.5 1.3 multiply_add_fusion.1
  38.8 1.2 copy.116
  40.0 1.3 multiply_subtract_fusion.1
  41.3 1.2 copy.113
  42.6 2.5 pad_maximum_fusion
  45.0 271.2 %all-reduce.6.cloned.1.call-done = f32[1024,2,512]{2,0,1:T(8,128)} async-done(((f32[1024,2,512]{2,0,1:T(8,128)}), f32[1024,2,512]{2,0,1:T(8,128)}) %all-reduce.6.cloned.1.call-update) | async-done | bytes 4194320
  317.3 1.3 fusion.32
  319.2 4.1 stack.57
  323.3 11.4 %all-to-all-start = ((f32[256,4,2,512]{3,2,1,0:T(2,128)}), f32[256,4,2,512]{3,2,1,0:T(2,128)}, u32[]{:S(2)}, u32[]{:S(2)}) async-start(f32[256,4,2,512]{3,2,1,0:T(2,128)} %stack.57), calls=%async_computation | async-start | bytes 8388608 | tf_op jit(solution)/shard_map/all_to_all | solution.py:133
  335.2 6.7 fusion.101
  341.9 87.1 %all-to-all-done = f32[256,4,2,512]{3,2,1,0:T(2,128)} async-done(((f32[256,4,2,512]{3,2,1,0:T(2,128)}), f32[256,4,2,512]{3,2,1,0:T(2,128)}, u32[]{:S(2)}, u32[]{:S(2)}) %all-to-all-start) | async-done | bytes 4194336 | tf_op jit(solution)/shard_map/all_to_all | solution.py:133
  429.0 7.8 fusion.331
  436.8 1.8 fusion.14
  438.6 1.7 fusion.15
  440.3 1.8 fusion.24
  442.1 1.9 fusion.25
  445.5 1.6 fusion.28
  447.1 1.6 fusion.29
  448.6 1.6 copy.123
  450.3 2.4 copy.124
  452.6 1.6 copy.127
  454.3 2.4 copy.128
  456.7 5.2 fusion.69
  461.9 13.3 %convert_reduce_fusion = (f32[32]{0:T(128)S(1)}, bf16[8,32,32,256]{3,2,1,0:T(8,128)(2,1)S(1)}) fusion(f32[32]{0:T(128)S(1)} %copy-done.9, f32[32,8,32,256]{3,0,2,1:T(8,128)} %fusion.101, f32[8,32,32,256]{3,2,1,0:T(8,128)S(1)} %fusion.69, f32[8,32,32,16]{2,3,1,0:T(8,128)S(1)} %copy-done.7, f32[16]{0:T(128)S(1)} %compare_select_fusion.1, ...), kind=kOutput, calls=%fused_computation.18 | convolution fusion | flops 258011104 | bytes 25690432 | tf_op jit(solution)/shard_map/abck,kz->abcz/dot_general | solution.py:11
  475.2 6.9 convolution_negate_fusion
  482.1 5.6 fusion.12
  487.7 3.9 copy.133
  491.5 2.9 convolution_multiply_fusion.1
  494.5 1.3 convolution_multiply_fusion
  495.8 1.3 convolution_subtract_fusion
  497.4 1.3 convolution_add_fusion
  498.8 1.2 fusion.44
  501.1 1.3 multiply_add_fusion
  502.4 1.2 copy.145
  503.6 1.3 multiply_subtract_fusion
  504.9 1.2 copy.142
  506.2 2.4 pad_maximum_fusion.1
  508.6 266.3 %all-reduce.8.cloned.1.call-done = f32[1024,2,512]{2,0,1:T(8,128)} async-done(((f32[1024,2,512]{2,0,1:T(8,128)}), f32[1024,2,512]{2,0,1:T(8,128)}) %all-reduce.8.cloned.1.call-update) | async-done | bytes 4194320
  777.9 4.1 stack.64
  782.0 11.4 %all-to-all-start.1 = ((f32[256,4,2,512]{3,2,1,0:T(2,128)}), f32[256,4,2,512]{3,2,1,0:T(2,128)}, u32[]{:S(2)}, u32[]{:S(2)}) async-start(f32[256,4,2,512]{3,2,1,0:T(2,128)} %stack.64), calls=%async_computation.1 | async-start | bytes 8388608 | tf_op jit(solution)/shard_map/all_to_all | solution.py:133
  793.4 4.7 convolution_bitcast_fusion.1
  798.1 130.5 %all-reduce.2 = (f32[32,32]{0,1:T(8,128)S(1)}, f32[32]{0:T(128)S(1)}) all-reduce(f32[32,32]{0,1:T(8,128)S(1)} %convolution_bitcast_fusion.1, f32[32]{0:T(128)S(1)} %get-tuple-element.40), channel_id=1, replica_groups=mesh['wide'=32,'narrow'=8] {'wide','narrow'}, use_global_device_ids=true, to_apply=%region_2.3 | all-reduce | flops 1056 | bytes 8448 | tf_op jit(solution)/shard_map/psum | solution.py:178
  929.7 6.6 fusion.99
  937.0 1.6 pad_maximum_fusion.2
  938.6 7.8 fusion.330
  946.4 1.8 fusion.18
  948.2 1.7 fusion.19
  949.9 1.8 fusion.22
  951.7 1.9 fusion.23
  956.7 1.9 copy.152
  958.7 2.6 copy.153
  961.3 1.9 copy.156
  963.2 3.4 copy.157
  966.6 3.5 fusion.74
  970.2 7.6 fusion.10
  (74 shorter events, 14.4 us)
Async XLA Ops:
  7.2 328.0 %copy-start = (bf16[32,32]{1,0:T(8,128)(2,1)S(1)}, bf16[32,32]{1,0:T(8,128)(2,1)}, u32[]{:S(2)}) copy-start(bf16[32,32]{1,0:T(8,128)(2,1)} %param.7) | copy-start | bytes 6148
  7.2 309.1 %all-reduce.6.cloned.1.call-start = ((), (), s32[]{:S(2)}) async-start(), calls=%async_computation.2 | async-start | bytes 8388608
  7.2 9.2 copy-start.1
  29.5 1.6 copy-start.4
  45.0 272.3 %copy-start.6 = (bf16[2,1,4,16,32,32]{5,4,3,2,1,0:T(8,128)(2,1)S(1)}, bf16[2,1,4,16,32,32]{5,4,3,2,1,0:T(8,128)(2,1)}, u32[]{:S(2)}) copy-start(bf16[2,1,4,16,32,32]{5,4,3,2,1,0:T(8,128)(2,1)} %param.9) | copy-start | bytes 786436
  323.3 105.7 %all-to-all-start = ((f32[256,4,2,512]{3,2,1,0:T(2,128)}), f32[256,4,2,512]{3,2,1,0:T(2,128)}, u32[]{:S(2)}, u32[]{:S(2)}) async-start(f32[256,4,2,512]{3,2,1,0:T(2,128)} %stack.57), calls=%async_computation | async-start | bytes 8388608 | tf_op jit(solution)/shard_map/all_to_all | solution.py:133
  334.7 440.1 %all-reduce.8.cloned.1.call-start = ((), (), s32[]{:S(2)}) async-start(), calls=%async_computation.3 | async-start | bytes 8388608
  456.6 5.2 copy-start.7
  456.6 5.3 copy-start.8
  456.7 5.3 copy-start.9
  475.2 6.9 copy-start.2
  495.8 1.6 copy-start.3
  782.0 156.6 %all-to-all-start.1 = ((f32[256,4,2,512]{3,2,1,0:T(2,128)}), f32[256,4,2,512]{3,2,1,0:T(2,128)}, u32[]{:S(2)}, u32[]{:S(2)}) async-start(f32[256,4,2,512]{3,2,1,0:T(2,128)} %stack.64), calls=%async_computation.1 | async-start | bytes 8388608 | tf_op jit(solution)/shard_map/all_to_all | solution.py:133
  966.6 3.5 copy-start.5
Sparse Core Ops, SparseCore 0:
  45.2 271.0 all-reduce.5
  508.7 266.1 all-reduce.7
